TPU v7x, 256 devices: a whole 4x4x8 slice. The times are simulated.
256 devices in a mesh: row: 32 (over z, x_lo, core), col: 8 (over x_hi, y).
Axes of the slice: x: 4 (x_hi: 2, x_lo: 2; x = x_hi * 2 + x_lo), y: 4, z: 8, core: 2. Of those that a mesh axis runs over, the one named last changes fastest.
Arguments:
- object_slices: float32 [2, 2, 3072, 768], P(None, None, 'row', 'col'), may hold values from -4 to 4
- probe: float32 [2, 192, 192], replicated, may hold values from -4 to 4
- propagator_phase: float32 [192, 192], replicated, may hold values from -3.140625 to 3.140625
- measured: float32 [32, 8, 2, 192, 192], P('row', 'col'), may hold values from 0 to 2
- offsets: int32 [32, 8, 2, 2], P('row', 'col'), may hold values from 0 to 95
- counts: int32 [32, 8], P('row', 'col'), may hold values from 1 to 2
Outputs:
- object_out: float32 [2, 2, 3072, 768], P(None, None, 'row', 'col')
- probe_out: float32 [2, 192, 192], replicated
Inputs may be any that keep to these rules, and one draw needn't show every extreme that they name: The slots below counts hold the tile's scan positions; the others are unused.
All inputs are finite; a program needn't handle non-finite values.
Results may differ from a plain program's by a relative error of at most 0.00014.
Values sent between devices are 32-bit elements; how exact they have to be, the bound alone decides.
A program may use at most 64 MiB of HBM per device.

v0:
```python
import math

import jax
import jax.numpy as jnp
from jax import lax
from jax.sharding import PartitionSpec as P

object_rate = 0.02
probe_rate = 0.3


def extended(cells, sides, width):
    for axis, dim in sides:
        count = lax.axis_size(axis)
        ends = count - 1
        head = lax.slice_in_dim(cells, 0, width, axis=dim)
        tail = lax.slice_in_dim(cells, cells.shape[dim] - width, cells.shape[dim], axis=dim)
        cells = jnp.concatenate(
            [
                lax.ppermute(tail, axis, [(i, (i + 1) % count) for i in range(ends)]),
                cells,
                lax.ppermute(head, axis, [((i + 1) % count, i) for i in range(ends)]),
            ],
            axis=dim,
        )
    return cells


def passed_along(x, axis, by):
    peers = lax.axis_size(axis)
    pairs = [(i, i + by) for i in range(peers) if 0 <= i + by < peers]
    return lax.ppermute(x, axis, pairs)


def times(a_real, a_imag, b_real, b_imag):
    return (a_real * b_real - a_imag * b_imag, a_real * b_imag + a_imag * b_real)


def times_conj(a_real, a_imag, b_real, b_imag):
    return (a_real * b_real + a_imag * b_imag, a_real * b_imag - a_imag * b_real)


def transform(x_real, x_imag, cosine, sine):
    highest = lax.Precision.HIGHEST

    def on_left(matrix, value):
        return jnp.einsum("jk,...kl->...jl", matrix, value, precision=highest)

    def on_right(value, matrix):
        return jnp.einsum("...jk,kl->...jl", value, matrix, precision=highest)

    mid_real = on_left(cosine, x_real) - on_left(sine, x_imag)
    mid_imag = on_left(cosine, x_imag) + on_left(sine, x_real)
    out_real = on_right(mid_real, cosine) - on_right(mid_imag, sine)
    out_imag = on_right(mid_imag, cosine) + on_right(mid_real, sine)
    return (out_real, out_imag)


def shards(object_slices, probe, propagator_phase, measured, offsets, counts):
    tile = object_slices.shape[-1]
    width = probe.shape[-1]
    slots = measured.shape[2]
    devices = lax.axis_size("row") * lax.axis_size("col")
    indices = jnp.arange(width, dtype=jnp.int32)
    products = indices[:, None] * indices[None, :] % width
    angles = products.astype(jnp.float32) * (2.0 * math.pi / width)
    norm_scale = 1.0 / math.sqrt(width)
    cosine = jnp.cos(angles) * norm_scale
    sine = jnp.sin(angles) * norm_scale
    minus_sine = -sine
    trans_real = jnp.cos(propagator_phase)
    trans_imag = jnp.sin(propagator_phase)
    intensities = measured[0, 0]
    starts = offsets[0, 0] + (tile - width // 2)
    live = counts[0, 0]
    zero = jnp.zeros((), jnp.int32)
    current = object_slices
    wave = probe
    padded = extended(current, (("row", 2), ("col", 3)), tile)
    wave_real = wave[0]
    wave_imag = wave[1]

    def process_position(row_offset, column_offset, measured_intensity):
        object_window = lax.dynamic_slice(
            padded, (zero, zero, row_offset, column_offset), (2, 2, width, width)
        )
        entry_real, entry_imag = times(
            wave_real, wave_imag, object_window[0, 0], object_window[0, 1]
        )
        spec_real, spec_imag = transform(entry_real, entry_imag, cosine, minus_sine)
        spec_real, spec_imag = times(trans_real, trans_imag, spec_real, spec_imag)
        carried_real, carried_imag = transform(spec_real, spec_imag, cosine, sine)
        leave_real, leave_imag = times(
            carried_real, carried_imag, object_window[1, 0], object_window[1, 1]
        )
        detector_real, detector_imag = transform(leave_real, leave_imag, cosine, minus_sine)
        amplitude_residual = (
            detector_real * detector_real + detector_imag * detector_imag - measured_intensity
        )
        back_real, back_imag = transform(
            amplitude_residual * detector_real, amplitude_residual * detector_imag, cosine, sine
        )
        second_real, second_imag = times_conj(carried_real, carried_imag, back_real, back_imag)
        before_real, before_imag = times_conj(
            object_window[1, 0], object_window[1, 1], back_real, back_imag
        )
        before_real, before_imag = transform(before_real, before_imag, cosine, minus_sine)
        before_real, before_imag = times_conj(trans_real, trans_imag, before_real, before_imag)
        inner_real, inner_imag = transform(before_real, before_imag, cosine, sine)
        first_real, first_imag = times_conj(wave_real, wave_imag, inner_real, inner_imag)
        grad_real, grad_imag = times_conj(
            object_window[0, 0], object_window[0, 1], inner_real, inner_imag
        )
        object_term = jnp.stack(
            [jnp.stack([first_real, first_imag]), jnp.stack([second_real, second_imag])]
        )
        return (object_term, jnp.stack([grad_real, grad_imag]))

    grad_pad = jnp.zeros(padded.shape, jnp.float32)
    wave_gradient = jnp.zeros(wave.shape, jnp.float32)
    object_terms, wave_terms = jax.vmap(process_position)(starts[:, 0], starts[:, 1], intensities)
    for slot in range(slots):
        position_weight = (slot < live).astype(jnp.float32)
        corner = (zero, zero, starts[slot, 0], starts[slot, 1])
        previous = lax.dynamic_slice(grad_pad, corner, (2, 2, width, width))
        grad_pad = lax.dynamic_update_slice(
            grad_pad, previous + position_weight * object_terms[slot], corner
        )
        wave_gradient = wave_gradient + position_weight * wave_terms[slot]
    from_right = passed_along(grad_pad[:, :, :, :tile], "col", -1)
    from_left = passed_along(grad_pad[:, :, :, 2 * tile :], "col", 1)
    folded = grad_pad[:, :, :, tile : 2 * tile] + from_right + from_left
    from_below = passed_along(folded[:, :, :tile], "row", -1)
    from_above = passed_along(folded[:, :, 2 * tile :], "row", 1)
    grad_object = folded[:, :, tile : 2 * tile] + from_below + from_above
    current = current - object_rate * grad_object
    rate = probe_rate / (slots * devices)
    total = lax.psum(wave_gradient, ("row", "col"))
    wave = wave - rate * total
    return (current, wave)


def solution(mesh):
    return jax.shard_map(
        shards,
        mesh=mesh,
        in_specs=(
            P(None, None, "row", "col"),
            P(),
            P(),
            P("row", "col", None, None, None),
            P("row", "col", None, None),
            P("row", "col"),
        ),
        out_specs=(P(None, None, "row", "col"), P()),
        check_vma=False,
    )
```

profile of v0, /device:TPU:1, one launch (start us, length us, event | category | flops | bytes accessed | tf_op | source)
XLA Modules:
  0.0 411.4 jit_solution(2080175894243225757)
XLA Ops:
  7.2 5.3 %collective-permute-start.1 = (f32[2,2,96,96]{3,2,1,0:T(8,128)}, f32[2,2,96,96]{3,2,1,0:T(8,128)S(1)}, u32[]{:S(2)}, u32[]{:S(2)}) collective-permute-start(f32[2,2,96,96]{3,2,1,0:T(8,128)} %param.6), channel_id=1, source_target_pairs={{8,0},{16,8},{24,16},{32,24},{40,32},{48,40},{56,48},{64,56},{72,6... | collective-permute-start | bytes 442376 | tf_op jit(solution)/shard_map/ppermute | solution.py:22
  12.5 1.9 collective-permute-start
  14.4 1.4 fusion.379
  21.6 1.6 fusion.378
  28.9 4.0 collective-permute-start.2
  33.0 10.8 %collective-permute-done.3 = f32[2,2,288,96]{3,2,1,0:T(8,128)S(1)} collective-permute-done((f32[2,2,288,96]{3,2,1,0:T(8,128)S(1)}, f32[2,2,288,96]{3,2,1,0:T(8,128)S(1)}, u32[]{:S(2)}, u32[]{:S(2)}) %collective-permute-start.3) | collective-permute-done | bytes 442400 | tf_op jit(solution)/shard_map/ppermute | solution.py:22
  45.4 6.7 %while.1 = (s32[]{:T(128)}, f32[2,2,288,288]{3,2,1,0:T(8,128)S(1)}, s32[2,4]{1,0:T(2,128)S(1)}, f32[2,2,2,192,192]{4,3,0,2,1:T(8,128)}, s32[]{:T(128)}) while((s32[]{:T(128)}, f32[2,2,288,288]{3,2,1,0:T(8,128)S(1)}, s32[2,4]{1,0:T(2,128)S(1)}, f32[2,2,2,192,192]{4,3,0,2,1:T(8,128)}, s32[]{:T(128)}) %tuple.40), condition=%wide.while_cond, body=%wide.while_body.sunk | while | flops 2 | bytes 1377405 | solution.py:84
  46.1 2.5 bitcast_dynamic-update-slice_fusion.2
  49.3 2.5 bitcast_dynamic-update-slice_fusion.2
  52.1 2.6 fusion.109
  54.6 2.4 fusion.105
  66.1 1.9 fusion.28
  78.3 1.5 convolution_subtract_fusion.7
  91.4 1.6 convolution_subtract_fusion.5
  103.2 1.7 fusion.77
  116.6 2.4 fusion.33
  120.2 7.8 %dynamic_update_slice.6 = f32[2,2,288,288]{3,2,1,0:T(8,128)S(1)} dynamic-update-slice(f32[2,2,288,288]{3,2,1,0:T(8,128)S(1)} %broadcast_in_dim.2, f32[2,2,192,192]{3,2,1,0:T(8,128)} %fusion.7, s32[]{:T(128)} %constant.13.clone.1, s32[]{:T(128)} %constant.13.clone.1, s32[]{:T(128)S(6)} %select_n.126, s32[]{:T(128)S(6)} %select_n.127) | dynamic-update-slice | bytes 1179652 | tf_op jit(solution)/shard_map/dynamic_update_slice | solution.py:126
  129.2 7.6 %dynamic_update_slice.7 = f32[2,2,288,288]{3,2,1,0:T(8,128)S(1)} dynamic-update-slice(f32[2,2,288,288]{3,2,1,0:T(8,128)S(1)} %dynamic_update_slice.6, f32[2,2,192,192]{3,2,1,0:T(8,128)} %fusion.10, s32[]{:T(128)} %constant.13.clone.1, s32[]{:T(128)} %constant.13.clone.1, s32[]{:T(128)S(6)} %select_n.128, s32[]{:T(128)S(6)} %select_n.129) | dynamic-update-slice | bytes 1179652 | tf_op jit(solution)/shard_map/dynamic_update_slice | solution.py:126
  139.1 5.4 %collective-permute-start.5 = (f32[2,2,288,96]{3,2,1,0:T(8,128)S(1)}, f32[2,2,288,96]{3,2,1,0:T(8,128)}, u32[]{:S(2)}, u32[]{:S(2)}) collective-permute-start(f32[2,2,288,96]{3,2,1,0:T(8,128)S(1)} %get-tuple-element.27), channel_id=1, source_target_pairs={{0,1},{1,2},{2,3},{3,4},{4,5},{5,6},{6,7},{8,9},{9,10},{10,11},{11... | collective-permute-start | bytes 1327112 | tf_op jit(solution)/shard_map/ppermute | solution.py:32
  145.5 8.5 %collective-permute-done.4 = f32[2,2,288,96]{3,2,1,0:T(8,128)S(1)} collective-permute-done((f32[2,2,288,96]{3,2,1,0:T(8,128)}, f32[2,2,288,96]{3,2,1,0:T(8,128)S(1)}, u32[]{:S(2)}, u32[]{:S(2)}) %collective-permute-start.4) | collective-permute-done | bytes 442400 | tf_op jit(solution)/shard_map/ppermute | solution.py:32
  156.0 4.6 %collective-permute-start.6 = (f32[2,2,96,96]{3,2,1,0:T(8,128)S(1)}, f32[2,2,96,96]{3,2,1,0:T(8,128)S(1)}, u32[]{:S(2)}, u32[]{:S(2)}) collective-permute-start(f32[2,2,96,96]{3,2,1,0:T(8,128)S(1)} %get-tuple-element.34), channel_id=1, source_target_pairs={{8,0},{16,8},{24,16},{32,24},{40,32},{48,40},{56,48},{64,56},{72,6... | collective-permute-start | bytes 442376 | tf_op jit(solution)/shard_map/ppermute | solution.py:32
  160.7 3.7 collective-permute-start.7
  164.4 237.5 %all-reduce.2.cloned.1.call-done = f32[2,192,192]{2,1,0:T(8,128)} async-done(((f32[2,192,192]{2,1,0:T(8,128)}), f32[2,192,192]{2,1,0:T(8,128)}) %all-reduce.2.cloned.1.call-update) | async-done | bytes 294928 | tf_op jit(solution)/shard_map/psum | solution.py:138
  401.8 1.8 multiply_subtract_fusion
  (91 shorter events, 67.0 us)
Async XLA Ops:
  7.2 25.8 %copy-start.4 = (f32[2,192,192]{2,1,0:T(8,128)S(1)}, f32[2,192,192]{2,1,0:T(8,128)}, u32[]{:S(2)}) copy-start(f32[2,192,192]{2,1,0:T(8,128)} %param.7) | copy-start | bytes 884740
  7.2 394.7 %all-reduce.2.cloned.1.call-start = ((), (), s32[]{:S(2)}) async-start(), calls=%async_computation | async-start | bytes 786432 | tf_op jit(solution)/shard_map/psum | solution.py:138
  7.2 20.3 %collective-permute-start.1 = (f32[2,2,96,96]{3,2,1,0:T(8,128)}, f32[2,2,96,96]{3,2,1,0:T(8,128)S(1)}, u32[]{:S(2)}, u32[]{:S(2)}) collective-permute-start(f32[2,2,96,96]{3,2,1,0:T(8,128)} %param.6), channel_id=1, source_target_pairs={{8,0},{16,8},{24,16},{32,24},{40,32},{48,40},{56,48},{64,56},{72,6... | collective-permute-start | bytes 442376 | tf_op jit(solution)/shard_map/ppermute | solution.py:22
  12.5 14.0 %collective-permute-start = (f32[2,2,96,96]{3,2,1,0:T(8,128)}, f32[2,2,96,96]{3,2,1,0:T(8,128)S(1)}, u32[]{:S(2)}, u32[]{:S(2)}) collective-permute-start(f32[2,2,96,96]{3,2,1,0:T(8,128)} %param.6), channel_id=1, source_target_pairs={{0,8},{8,16},{16,24},{24,32},{32,40},{40,48},{48,56},{56,64},{64,7... | collective-permute-start | bytes 442376 | tf_op jit(solution)/shard_map/ppermute | solution.py:20
  27.6 16.3 %collective-permute-start.3 = (f32[2,2,288,96]{3,2,1,0:T(8,128)S(1)}, f32[2,2,288,96]{3,2,1,0:T(8,128)S(1)}, u32[]{:S(2)}, u32[]{:S(2)}) collective-permute-start(f32[2,2,288,96]{3,2,1,0:T(8,128)S(1)} %constant_dynamic-update-slice_fusion), channel_id=1, source_target_pairs={{1,0},{2,1},{3,2},{4,3},{5,4},{6,5},{7,6},{9,8},{10,9},{11,10},{12... | collective-permute-start | bytes 1327112 | tf_op jit(solution)/shard_map/ppermute | solution.py:22
  28.9 15.8 %collective-permute-start.2 = (f32[2,2,288,96]{3,2,1,0:T(8,128)S(1)}, f32[2,2,288,96]{3,2,1,0:T(8,128)S(1)}, u32[]{:S(2)}, u32[]{:S(2)}) collective-permute-start(f32[2,2,288,96]{3,2,1,0:T(8,128)S(1)} %constant_dynamic-update-slice_fusion), channel_id=1, source_target_pairs={{0,1},{1,2},{2,3},{3,4},{4,5},{5,6},{6,7},{8,9},{9,10},{10,11},{11... | collective-permute-start | bytes 1327112 | tf_op jit(solution)/shard_map/ppermute | solution.py:20
  52.1 5.0 %copy-start.1 = (f32[2,2,2,192,192]{4,3,0,2,1:T(8,128)S(1)}, f32[2,2,2,192,192]{4,3,0,2,1:T(8,128)}, u32[]{:S(2)}) copy-start(f32[2,2,2,192,192]{4,3,0,2,1:T(8,128)} %get-tuple-element.9) | copy-start | bytes 3538948
  82.3 3.8 copy-start
  136.8 7.8 %copy-start.2 = (f32[1,2,192,192]{3,2,1,0:T(8,128)S(1)}, f32[1,2,192,192]{3,2,1,0:T(8,128)}, u32[]{:S(2)}) copy-start(f32[1,2,192,192]{3,2,1,0:T(8,128)} %get-tuple-element.20) | copy-start | bytes 884740
  136.8 7.8 %copy-start.3 = (f32[1,2,192,192]{3,2,1,0:T(8,128)S(1)}, f32[1,2,192,192]{3,2,1,0:T(8,128)}, u32[]{:S(2)}) copy-start(f32[1,2,192,192]{3,2,1,0:T(8,128)} %get-tuple-element.21) | copy-start | bytes 884740
  137.9 16.1 %collective-permute-start.4 = (f32[2,2,288,96]{3,2,1,0:T(8,128)}, f32[2,2,288,96]{3,2,1,0:T(8,128)S(1)}, u32[]{:S(2)}, u32[]{:S(2)}) collective-permute-start(f32[2,2,288,96]{3,2,1,0:T(8,128)} %get-tuple-element.26), channel_id=1, source_target_pairs={{1,0},{2,1},{3,2},{4,3},{5,4},{6,5},{7,6},{9,8},{10,9},{11,10},{12... | collective-permute-start | bytes 1327112 | tf_op jit(solution)/shard_map/ppermute | solution.py:32
  139.1 15.5 %collective-permute-start.5 = (f32[2,2,288,96]{3,2,1,0:T(8,128)S(1)}, f32[2,2,288,96]{3,2,1,0:T(8,128)}, u32[]{:S(2)}, u32[]{:S(2)}) collective-permute-start(f32[2,2,288,96]{3,2,1,0:T(8,128)S(1)} %get-tuple-element.27), channel_id=1, source_target_pairs={{0,1},{1,2},{2,3},{3,4},{4,5},{5,6},{6,7},{8,9},{9,10},{10,11},{11... | collective-permute-start | bytes 1327112 | tf_op jit(solution)/shard_map/ppermute | solution.py:32
  145.5 256.4 %copy-start.5 = (f32[2,192,192]{2,1,0:T(8,128)S(1)}, f32[2,192,192]{2,1,0:T(8,128)}, u32[]{:S(2)}) copy-start(f32[2,192,192]{2,1,0:T(8,128)} %param.7) | copy-start | bytes 884740
  156.0 247.7 %copy-start.6 = (f32[2,2,96,96]{3,2,1,0:T(8,128)S(1)}, f32[2,2,96,96]{3,2,1,0:T(8,128)}, u32[]{:S(2)}) copy-start(f32[2,2,96,96]{3,2,1,0:T(8,128)} %param.6) | copy-start | bytes 442372
  156.0 247.6 %collective-permute-start.6 = (f32[2,2,96,96]{3,2,1,0:T(8,128)S(1)}, f32[2,2,96,96]{3,2,1,0:T(8,128)S(1)}, u32[]{:S(2)}, u32[]{:S(2)}) collective-permute-start(f32[2,2,96,96]{3,2,1,0:T(8,128)S(1)} %get-tuple-element.34), channel_id=1, source_target_pairs={{8,0},{16,8},{24,16},{32,24},{40,32},{48,40},{56,48},{64,56},{72,6... | collective-permute-start | bytes 442376 | tf_op jit(solution)/shard_map/ppermute | solution.py:32
  160.7 243.0 %collective-permute-start.7 = (f32[2,2,96,96]{3,2,1,0:T(8,128)S(1)}, f32[2,2,96,96]{3,2,1,0:T(8,128)S(1)}, u32[]{:S(2)}, u32[]{:S(2)}) collective-permute-start(f32[2,2,96,96]{3,2,1,0:T(8,128)S(1)} %get-tuple-element.35), channel_id=1, source_target_pairs={{0,8},{8,16},{16,24},{24,32},{32,40},{40,48},{48,56},{56,64},{64,7... | collective-permute-start | bytes 442376 | tf_op jit(solution)/shard_map/ppermute | solution.py:32
Sparse Core Ops, SparseCore 0:
  145.6 256.2 all-reduce.1
where the time goes:
time: 415 us; the launch traced here: 411 us
  waiting for transfers between devices  258 us (62%)
  matrix products  66.4 us (16%)
  starting transfers between devices  27.6 us (7%)
  local copies, waits for them, and re-layouts  27.1 us (7%)
  between operations  23 us (6%)
  other arithmetic  8.58 us (2%)
    psum x1, waiting for transfers between devices, shards(): total = lax.psum(wave_gradient, ('row', 'col'))  237 us
    dot_general x24, matrix products, on_left(): return jnp.einsum('jk,...kl->...jl', matrix, value, precision=highest)  35 us
    dot_general x24, matrix products, on_right(): return jnp.einsum('...jk,kl->...jl', value, matrix, precision=highest)  31.4 us
    dynamic_update_slice x2, local copies, waits for them, and re-layouts, shards(): lax.dynamic_update_slice(grad_pad, previous + position_weight * object_te...  15.4 us
    ppermute x4, starting transfers between devices, passed_along(): return lax.ppermute(x, axis, pairs)  15.1 us
    ppermute x2, waiting for transfers between devices, extended(): lax.ppermute(head, axis, [((i + 1) % count, i) for i in range(ends)])  10.8 us
    ppermute x4, waiting for transfers between devices, passed_along(): return lax.ppermute(x, axis, pairs)  9.2 us
  transfers between devices with their start and end apart: 9, of which 5 were waited for; matrix products, arithmetic and copies ran while one was open for 2% of the time, Pallas kernels for 0%

commit v1 on v0

v1 whole, which is shorter than its diff:
```python
import functools

import jax
import jax.numpy as jnp
import ml_dtypes
import numpy as np
from jax import lax
from jax.experimental import pallas as pl
from jax.experimental.pallas import tpu as pltpu
from jax.sharding import PartitionSpec as P

OBJECT_RATE = 0.02
PROBE_RATE = 0.3
TILE = 96
WIDTH = 192
LANES = 256
SLOTS = 2
HALF = 288
MESH = pl.DeviceIdType.MESH
AROUND = [(i, j) for i in (-1, 0, 1) for j in (-1, 0, 1) if (i, j) != (0, 0)]
F32 = jnp.float32
BF16 = jnp.bfloat16


def place(i, j):
    return (i + 1) * 3 + (j + 1)


def matrices():
    n = np.arange(WIDTH)
    angle = 2.0 * np.pi * (np.outer(n, n) % WIDTH) / WIDTH
    c = np.cos(angle) / np.sqrt(WIDTH)
    s = np.sin(angle) / np.sqrt(WIDTH)
    right = np.zeros((2 * LANES, 2 * LANES))
    right[:WIDTH, :WIDTH] = c
    right[:WIDTH, LANES : LANES + WIDTH] = -s
    right[LANES : LANES + WIDTH, :WIDTH] = s
    right[LANES : LANES + WIDTH, LANES : LANES + WIDTH] = c
    left = np.block([[c, s], [-s, c]])
    parts = []
    for full in (right, left):
        high = full.astype(np.float32).astype(ml_dtypes.bfloat16)
        low = (full - high.astype(np.float64)).astype(np.float32).astype(ml_dtypes.bfloat16)
        parts += [high, low]
    return parts


def two(x):
    high = x.astype(BF16)
    return high, (x - high.astype(F32)).astype(BF16)


def times(ar, ai, br, bi):
    return ar * br - ai * bi, ar * bi + ai * br


def times_conj(ar, ai, br, bi):
    return ar * br + ai * bi, ar * bi - ai * br


def dot(a, b):
    return jnp.dot(a, b, preferred_element_type=F32)


def chunks(body, step, total=WIDTH):
    def run(i, carry):
        body(pl.multiple_of(i * step, step))
        return carry

    lax.fori_loop(0, total // step, run, 0)


def kernel(
    rows, cols, share, owners,
    offsets, counts, obj, probe, phase, measured, wrh, wrl, wlh, wll,
    obj_out, probe_out,
    own, halo, band, win, wave, trans, xh, xl, lh, ll, y, carried, shift,
    gsend, grecv, pack, half_in, plane_in, deep_in, total,
    halo_s, halo_r, grad_s, grad_r, pair_s, pair_r, plane_s, plane_r, deep_s, deep_r,
    back_s, back_r, last_s, last_r,
):
    r = lax.axis_index("row")
    c = lax.axis_index("col")
    core = lax.rem(r, 2)
    x_lo = lax.rem(lax.div(r, 2), 2)
    z = lax.div(r, 4)
    depth = rows // 4
    group = 2 * cols
    me = x_lo * cols + c
    other = (r + 1 - 2 * core, c)

    def beside(i, j):
        return (lax.rem(r + i + rows, rows), lax.rem(c + j + cols, cols))

    def in_plane(p):
        return (z * 4 + (p // cols) * 2 + core, p % cols)

    def in_depth(k):
        return (k * 4 + x_lo * 2 + core, c)

    def inside(i, j):
        return (r + i >= 0) & (r + i < rows) & (c + j >= 0) & (c + j < cols)

    barrier = pltpu.get_barrier_semaphore()

    def greet(device):
        pl.semaphore_signal(barrier, inc=1, device_id=device, device_id_type=MESH)

    for i, j in AROUND:
        greet(beside(i, j))
    greet(other)
    for d in range(1, group):
        p = lax.rem(me + d, group)
        greet((z * 4 + lax.div(p, cols) * 2 + core, lax.rem(p, cols)))
    for d in range(1, depth):
        greet((lax.rem(z + d, depth) * 4 + x_lo * 2 + core, c))

    for s in range(2):
        for k in range(2):
            own[s, k] = jnp.zeros((TILE, 128), F32)
            own[s, k, :, :TILE] = obj[s, k]

    pl.semaphore_wait(barrier, len(AROUND) + group + depth - 1)

    def halo_copy(s, i, j):
        return pltpu.make_async_remote_copy(
            src_ref=own.at[s],
            dst_ref=halo.at[s, place(-i, -j)],
            send_sem=halo_s.at[s, place(i, j)],
            recv_sem=halo_r.at[s, place(-i, -j)],
            device_id=beside(i, j),
            device_id_type=MESH,
        )

    def grad_copy(s, i, j):
        return pltpu.make_async_remote_copy(
            src_ref=gsend.at[s, place(i, j)],
            dst_ref=grecv.at[s, place(-i, -j)],
            send_sem=grad_s.at[s, place(i, j)],
            recv_sem=grad_r.at[s, place(-i, -j)],
            device_id=beside(i, j),
            device_id_type=MESH,
        )

    for s in range(2):
        for i, j in AROUND:
            halo_copy(s, i, j).start()

    for k in range(2):
        wave[k] = jnp.zeros((WIDTH, LANES), F32)
        wave[k, :, :WIDTH] = probe[k]
        trans[k] = jnp.zeros((WIDTH, LANES), F32)
    trans[0, :, :WIDTH] = jnp.cos(phase[...])
    trans[1, :, :WIDTH] = jnp.sin(phase[...])
    for slot in range(SLOTS):
        for k in range(2):
            for m in range(2):
                shift[slot, k, m, :TILE] = jnp.zeros((TILE, 128), F32)
                shift[slot, k, m, TILE + WIDTH :] = jnp.zeros((TILE, 128), F32)

    ro = [offsets[0, 0, slot, 0] for slot in range(SLOTS)]
    co = [offsets[0, 0, slot, 1] for slot in range(SLOTS)]
    live = [slot < counts[0, 0] for slot in range(SLOTS)]

    def windows(s):
        for i in (-1, 0, 1):
            for k in range(2):
                pieces = []
                for j in (-1, 0, 1):
                    if (i, j) == (0, 0):
                        pieces.append(own[s, k])
                    else:
                        pieces.append(jnp.where(inside(i, j), halo[s, place(i, j), k], 0.0))
                lane = lax.broadcasted_iota(jnp.int32, (TILE, 128), 1)
                a = pieces[0]
                b = pltpu.roll(pieces[1], 96, 1)
                d = pltpu.roll(pieces[2], 64, 1)
                at = pl.ds((i + 1) * TILE, TILE)
                band[k, 0, at] = jnp.where(lane < 96, a, b)
                band[k, 1, at] = jnp.where(lane < 64, b, d)
                band[k, 2, at] = jnp.where(lane < 64, d, 0.0)
        for slot in range(SLOTS):
            for k in range(2):
                lane = lax.broadcasted_iota(jnp.int32, (WIDTH, 128), 1)
                turn = lax.rem(128 - co[slot], 128)
                at = pl.ds(ro[slot], WIDTH)
                v = [pltpu.roll(band[k, m, at], turn, 1) for m in range(3)]
                keep = lane < 128 - co[slot]
                win[s, slot, k, :, 0:128] = jnp.where(keep, v[0], v[1])
                win[s, slot, k, :, 128:256] = jnp.where(keep, v[1], v[2])

    def put(slot, at, step, re, im, inverse):
        if inverse:
            re, im = im, re
        to = pl.ds(slot * WIDTH + at, step)
        xh[to, :LANES], xl[to, :LANES] = two(re)
        xh[to, LANES:], xl[to, LANES:] = two(im)

    def transform():
        acc = dot(xh[...], wrh[...]) + dot(xl[...], wrh[...]) + dot(xh[...], wrl[...])
        for slot in range(SLOTS):
            part = acc[slot * WIDTH : (slot + 1) * WIDTH]
            lh[slot, :WIDTH], ll[slot, :WIDTH] = two(part[:, :LANES])
            lh[slot, WIDTH:], ll[slot, WIDTH:] = two(part[:, LANES:])
        for slot in range(SLOTS):
            y[slot] = (
                dot(wlh[...], lh[slot]) + dot(wlh[...], ll[slot]) + dot(wll[...], lh[slot])
            )

    def got(slot, at, step, inverse):
        one = y[slot, pl.ds(at, step), :]
        two_ = y[slot, pl.ds(WIDTH + at, step), :]
        return (two_, one) if inverse else (one, two_)

    step = 32

    def each(body):
        for slot in range(SLOTS):
            chunks(functools.partial(body, slot), step)

    def spread(s):
        for i in (-1, 0, 1):
            for k in range(2):
                lane = lax.broadcasted_iota(jnp.int32, (TILE, 128), 1)
                v = [0.0, 0.0, 0.0]
                for slot in range(SLOTS):
                    at = pl.ds(TILE * (i + 2) - ro[slot], TILE)
                    a = pltpu.roll(shift[slot, k, 0, at], co[slot], 1)
                    b = pltpu.roll(shift[slot, k, 1, at], co[slot], 1)
                    wrap = lane < co[slot]
                    v[0] = v[0] + jnp.where(wrap, 0.0, a)
                    v[1] = v[1] + jnp.where(wrap, a, b)
                    v[2] = v[2] + jnp.where(wrap, b, 0.0)
                gsend[s, place(i, -1), k] = v[0]
                gsend[s, place(i, 0), k] = jnp.where(
                    lane < 32, pltpu.roll(v[0], 32, 1), pltpu.roll(v[1], 32, 1)
                )
                gsend[s, place(i, 1), k] = jnp.where(
                    lane < 64, pltpu.roll(v[1], 64, 1), pltpu.roll(v[2], 64, 1)
                )

    def shifted(slot, at, re, im):
        to = pl.ds(TILE + at, step)
        for k, part in enumerate((re, im)):
            part = jnp.where(live[slot], part, 0.0)
            shift[slot, k, 0, to] = part[:, :128]
            shift[slot, k, 1, to] = part[:, 128:]

    for i, j in AROUND:
        halo_copy(0, i, j).wait_recv()
    windows(0)

    def enter(slot, at):
        d = pl.ds(at, step)
        re, im = times(wave[0, d], wave[1, d], win[0, slot, 0, d], win[0, slot, 1, d])
        put(slot, at, step, re, im, False)

    each(enter)
    transform()

    def carry(slot, at):
        d = pl.ds(at, step)
        re, im = got(slot, at, step, False)
        re, im = times(trans[0, d], trans[1, d], re, im)
        put(slot, at, step, re, im, True)

    each(carry)
    transform()

    for i, j in AROUND:
        halo_copy(1, i, j).wait_recv()
    windows(1)

    def leave(slot, at):
        d = pl.ds(at, step)
        re, im = got(slot, at, step, True)
        carried[slot, 0, d] = re
        carried[slot, 1, d] = im
        re, im = times(re, im, win[1, slot, 0, d], win[1, slot, 1, d])
        put(slot, at, step, re, im, False)

    each(leave)
    transform()

    def residual(slot, at):
        re, im = got(slot, at, step, False)
        seen = jnp.concatenate(
            [measured[slot, pl.ds(at, step), :], jnp.zeros((step, LANES - WIDTH), F32)], axis=1
        )
        resid = re * re + im * im - seen
        put(slot, at, step, resid * re, resid * im, True)

    each(residual)
    transform()

    def second(slot, at):
        d = pl.ds(at, step)
        re, im = got(slot, at, step, True)
        shifted(slot, at, *times_conj(carried[slot, 0, d], carried[slot, 1, d], re, im))
        re, im = times_conj(win[1, slot, 0, d], win[1, slot, 1, d], re, im)
        put(slot, at, step, re, im, False)

    each(second)
    spread(1)
    for i, j in AROUND:
        grad_copy(1, i, j).start()
    transform()

    def inner(slot, at):
        d = pl.ds(at, step)
        re, im = got(slot, at, step, False)
        re, im = times_conj(trans[0, d], trans[1, d], re, im)
        put(slot, at, step, re, im, True)

    each(inner)
    transform()

    def probe_part(at):
        d = pl.ds(at, step)
        re = jnp.zeros((step, LANES), F32)
        im = jnp.zeros((step, LANES), F32)
        for slot in range(SLOTS):
            ir, ii = got(slot, at, step, True)
            pr, pi = times_conj(win[0, slot, 0, d], win[0, slot, 1, d], ir, ii)
            re = re + jnp.where(live[slot], pr, 0.0)
            im = im + jnp.where(live[slot], pi, 0.0)
            shifted(slot, at, *times_conj(wave[0, d], wave[1, d], ir, ii))
        lane = lax.broadcasted_iota(jnp.int32, (step, 128), 1)
        pack[d] = re[:, :128]
        pack[pl.ds(WIDTH + at, step)] = im[:, :128]
        pack[pl.ds(2 * WIDTH + at, step)] = jnp.where(
            lane < 64, re[:, 128:], pltpu.roll(im[:, 128:], 64, 1)
        )

    chunks(probe_part, step)

    mine = pl.multiple_of(HALF * core, 8)
    theirs = pl.multiple_of(HALF * (1 - core), 8)
    pair = pltpu.make_async_remote_copy(
        src_ref=pack.at[pl.ds(theirs, HALF)],
        dst_ref=half_in,
        send_sem=pair_s,
        recv_sem=pair_r,
        device_id=other,
        device_id_type=MESH,
    )
    pair.start()

    spread(0)
    for i, j in AROUND:
        grad_copy(0, i, j).start()

    pair.wait_recv()
    half_in[...] = half_in[...] + pack[pl.ds(mine, HALF)]

    def plane_copy(q, sender):
        return pltpu.make_async_remote_copy(
            src_ref=half_in.at[pl.ds(q * share, share)],
            dst_ref=plane_in.at[sender],
            send_sem=plane_s.at[q],
            recv_sem=plane_r.at[sender],
            device_id=in_plane(q),
            device_id_type=MESH,
        )

    for q in range(owners):
        @pl.when(me != q)
        def _():
            plane_copy(q, me).start()

    for i, j in AROUND:
        grad_copy(1, i, j).wait_recv()

    def update(s):
        for k in range(2):
            whole = gsend[s, place(0, 0), k]
            for i, j in AROUND:
                whole = whole + jnp.where(inside(i, j), grecv[s, place(i, j), k], 0.0)
            obj_out[s, k] = obj[s, k] - OBJECT_RATE * whole[:, :TILE]

    update(1)

    my_share = pl.multiple_of(me * share, 8)

    def deep_copy(k, sender):
        return pltpu.make_async_remote_copy(
            src_ref=deep_in.at[z],
            dst_ref=deep_in.at[sender],
            send_sem=deep_s.at[k],
            recv_sem=deep_r.at[sender],
            device_id=in_depth(k),
            device_id_type=MESH,
        )

    @pl.when(me < owners)
    def _():
        whole = half_in[pl.ds(my_share, share)]
        for p in range(group):
            @pl.when(me != p)
            def _():
                plane_copy(0, p).wait_recv()
        plane_in[me] = whole
        whole = plane_in[0]
        for p in range(1, group):
            whole = whole + plane_in[p]
        deep_in[z] = whole
        for k in range(depth):
            @pl.when(z != k)
            def _():
                deep_copy(k, z).start()

    for i, j in AROUND:
        grad_copy(0, i, j).wait_recv()
    update(0)

    def back_copy(p, sender):
        at = pl.ds(pl.multiple_of(mine + sender * share, 8), share)
        return pltpu.make_async_remote_copy(
            src_ref=total.at[at],
            dst_ref=total.at[at],
            send_sem=back_s.at[p],
            recv_sem=back_r.at[sender],
            device_id=in_plane(p),
            device_id_type=MESH,
        )

    def last_copy(base, q):
        at = pl.ds(pl.multiple_of(base + q * share, 8), share)
        return pltpu.make_async_remote_copy(
            src_ref=total.at[at],
            dst_ref=total.at[at],
            send_sem=last_s.at[q],
            recv_sem=last_r.at[q],
            device_id=other,
            device_id_type=MESH,
        )

    @pl.when(me < owners)
    def _():
        for k in range(depth):
            @pl.when(z != k)
            def _():
                deep_copy(0, k).wait_recv()
        whole = deep_in[0]
        for k in range(1, depth):
            whole = whole + deep_in[k]
        total[pl.ds(pl.multiple_of(mine + my_share, 8), share)] = whole
        for p in range(group):
            @pl.when(me != p)
            def _():
                back_copy(p, me).start()

    for q in range(owners):
        @pl.when(me != q)
        def _():
            back_copy(0, q).wait_recv()
        last_copy(mine, q).start()
    for q in range(owners):
        last_copy(theirs, q).wait_recv()

    rate = PROBE_RATE / (SLOTS * rows * cols)

    def finish(at):
        d = pl.ds(at, step)
        re = total[d]
        im = total[pl.ds(WIDTH + at, step)]
        rest = total[pl.ds(2 * WIDTH + at, step)]
        probe_out[0, d, :128] = probe[0, d, :128] - rate * re
        probe_out[1, d, :128] = probe[1, d, :128] - rate * im
        probe_out[0, d, 128:] = probe[0, d, 128:] - rate * rest[:, :64]
        probe_out[1, d, 128:] = probe[1, d, 128:] - rate * pltpu.roll(rest, 64, 1)[:, :64]

    chunks(finish, step)

    for s in range(2):
        for i, j in AROUND:
            halo_copy(s, i, j).wait_send()
            grad_copy(s, i, j).wait_send()
    pair.wait_send()
    for q in range(owners):
        @pl.when(me != q)
        def _():
            plane_copy(q, me).wait_send()
        last_copy(mine, q).wait_send()

    @pl.when(me < owners)
    def _():
        for k in range(depth):
            @pl.when(z != k)
            def _():
                deep_copy(k, z).wait_send()
        for p in range(group):
            @pl.when(me != p)
            def _():
                back_copy(p, me).wait_send()


def solution(mesh):
    rows, cols = mesh.shape["row"], mesh.shape["col"]
    group, depth = 2 * cols, rows // 4
    share = -(-(HALF // 8) // group) * 8
    owners = HALF // share
    consts = matrices()

    def shards(object_slices, probe, propagator_phase, measured, offsets, counts):
        vmem = pl.BlockSpec(memory_space=pltpu.VMEM)
        smem = pl.BlockSpec(memory_space=pltpu.SMEM)
        dma = pltpu.SemaphoreType.DMA
        square = (WIDTH, LANES)
        return pl.pallas_call(
            functools.partial(kernel, rows, cols, share, owners),
            out_shape=(
                jax.ShapeDtypeStruct(object_slices.shape, F32),
                jax.ShapeDtypeStruct(probe.shape, F32),
            ),
            in_specs=[smem, smem] + [vmem] * 8,
            out_specs=(vmem, vmem),
            scratch_shapes=[
                pltpu.VMEM((2, 2, TILE, 128), F32),
                pltpu.VMEM((2, 9, 2, TILE, 128), F32),
                pltpu.VMEM((2, 3, 3 * TILE, 128), F32),
                pltpu.VMEM((2, SLOTS, 2) + square, F32),
                pltpu.VMEM((2,) + square, F32),
                pltpu.VMEM((2,) + square, F32),
                pltpu.VMEM((SLOTS * WIDTH, 2 * LANES), BF16),
                pltpu.VMEM((SLOTS * WIDTH, 2 * LANES), BF16),
                pltpu.VMEM((SLOTS, 2 * WIDTH, LANES), BF16),
                pltpu.VMEM((SLOTS, 2 * WIDTH, LANES), BF16),
                pltpu.VMEM((SLOTS, 2 * WIDTH, LANES), F32),
                pltpu.VMEM((SLOTS, 2) + square, F32),
                pltpu.VMEM((SLOTS, 2, 2, 4 * TILE, 128), F32),
                pltpu.VMEM((2, 9, 2, TILE, 128), F32),
                pltpu.VMEM((2, 9, 2, TILE, 128), F32),
                pltpu.VMEM((2 * HALF, 128), F32),
                pltpu.VMEM((HALF, 128), F32),
                pltpu.VMEM((group, share, 128), F32),
                pltpu.VMEM((depth, share, 128), F32),
                pltpu.VMEM((2 * HALF, 128), F32),
                dma((2, 9)), dma((2, 9)), dma((2, 9)), dma((2, 9)),
                dma, dma,
                dma((owners,)), dma((group,)),
                dma((depth,)), dma((depth,)),
                dma((group,)), dma((owners,)),
                dma((owners,)), dma((owners,)),
            ],
            compiler_params=pltpu.CompilerParams(
                collective_id=0, has_side_effects=True, vmem_limit_bytes=48 * 1024 * 1024
            ),
        )(
            offsets, counts, object_slices, probe, propagator_phase, measured[0, 0],
            *[jnp.asarray(m) for m in consts],
        )

    return jax.shard_map(
        shards,
        mesh=mesh,
        in_specs=(
            P(None, None, "row", "col"),
            P(),
            P(),
            P("row", "col", None, None, None),
            P("row", "col", None, None),
            P("row", "col"),
        ),
        out_specs=(P(None, None, "row", "col"), P()),
        check_vma=False,
    )
```

time: 415 us -> 82.4 us (0.20)
  waiting for transfers between devices: 258 us -> 0 us
  Pallas kernels: 0 us -> 70.8 us
  matrix products: 66.4 us -> 0 us
  starting transfers between devices: 27.6 us -> 0 us
  between operations: 23 us -> 1.3 us
  local copies, waits for them, and re-layouts: 27.1 us -> 9.94 us
  other arithmetic: 8.58 us -> 0 us
    psum x1 -> x0, waiting for transfers between devices: 237 us -> none  [shards(): total = lax.psum(wave_gradient, ('row', 'col'))]
    pallas_call x0 -> x1, Pallas kernels: none -> 70.8 us  [shards(): pl.pallas_call(functools.partial(kernel, rows, cols, share, owners), out_...]
    dot_general x48 -> x0, matrix products: 66.4 us -> none  [the longest x24 35 us: on_left(): return jnp.einsum('jk,...kl->...jl', matrix, value, precision=highest)]
    ppermute x8 -> x0, starting transfers between devices: 27.6 us -> none  [the longest x4 15.1 us: passed_along(): return lax.ppermute(x, axis, pairs)]
    ppermute x8 -> x0, waiting for transfers between devices: 20.9 us -> none  [the longest x2 10.8 us: extended(): lax.ppermute(head, axis, [((i + 1) % count, i) for i in range(ends)])]
    dynamic_update_slice x2 -> x0, local copies, waits for them, and re-layouts: 15.4 us -> none  [shards(): lax.dynamic_update_slice(grad_pad, previous + position_weight * object_te...]
    unnamed x16 -> x20, local copies, waits for them, and re-layouts: 1 us -> 9.94 us
    gather x6 -> x0, local copies, waits for them, and re-layouts: 6.39 us -> none
  transfers between devices with their start and end apart: 9 -> 0, of which waited for: 5 -> 0; matrix products, arithmetic and copies ran while one was open for 2% -> 0% of each run, Pallas kernels for 0% -> 0%
where the time goes in v1:
time: 82.4 us; the launch traced here: 82 us
  Pallas kernels  70.8 us (86%)
  local copies, waits for them, and re-layouts  9.94 us (12%)
  between operations  1.3 us (2%)
    pallas_call x1, Pallas kernels, shards(): pl.pallas_call(functools.partial(kernel, rows, cols, share, owners), out_...  70.8 us
    unnamed x20, local copies, waits for them, and re-layouts  9.94 us

profile of v1, /device:TPU:1, one launch (start us, length us, event | category | flops | bytes accessed | tf_op | source)
XLA Modules:
  0.0 82.0 jit_solution(14574937394320988345)
XLA Ops:
  1.3 0.0 copy-start.8
  1.3 0.7 copy-done.8
  2.0 0.0 copy-start
  2.0 1.0 %copy-done = bf16[512,512]{1,0:T(8,128)(2,1)S(1)} copy-done((bf16[512,512]{1,0:T(8,128)(2,1)S(1)}, bf16[512,512]{1,0:T(8,128)(2,1)}, u32[]{:S(2)}) %copy-start) | copy-done | bytes 524312
  3.0 0.0 copy-start.1
  3.0 1.0 %copy-done.1 = bf16[512,512]{1,0:T(8,128)(2,1)S(1)} copy-done((bf16[512,512]{1,0:T(8,128)(2,1)S(1)}, bf16[512,512]{1,0:T(8,128)(2,1)}, u32[]{:S(2)}) %copy-start.1) | copy-done | bytes 524312
  4.0 0.0 copy-start.2
  4.0 1.0 %copy-done.2 = f32[2,192,192]{2,1,0:T(8,128)S(1)} copy-done((f32[2,192,192]{2,1,0:T(8,128)S(1)}, f32[2,192,192]{2,1,0:T(8,128)}, u32[]{:S(2)}) %copy-start.2) | copy-done | bytes 294936
  5.0 0.0 copy-start.3
  5.0 1.0 %copy-done.3 = f32[1,1,2,192,192]{4,3,2,1,0:T(8,128)S(1)} copy-done((f32[1,1,2,192,192]{4,3,2,1,0:T(8,128)S(1)}, f32[1,1,2,192,192]{4,3,2,1,0:T(8,128)}, u32[]{:S(2)}) %copy-start.3) | copy-done | bytes 294936
  6.0 0.0 copy-start.4
  6.0 1.0 %copy-done.4 = bf16[384,384]{1,0:T(8,128)(2,1)S(1)} copy-done((bf16[384,384]{1,0:T(8,128)(2,1)S(1)}, bf16[384,384]{1,0:T(8,128)(2,1)}, u32[]{:S(2)}) %copy-start.4) | copy-done | bytes 294936
  7.0 0.0 copy-start.5
  7.0 1.0 %copy-done.5 = bf16[384,384]{1,0:T(8,128)(2,1)S(1)} copy-done((bf16[384,384]{1,0:T(8,128)(2,1)S(1)}, bf16[384,384]{1,0:T(8,128)(2,1)}, u32[]{:S(2)}) %copy-start.5) | copy-done | bytes 294936
  8.0 0.0 copy-start.6
  8.0 0.9 %copy-done.6 = f32[2,2,96,96]{3,2,1,0:T(8,128)S(1)} copy-done((f32[2,2,96,96]{3,2,1,0:T(8,128)S(1)}, f32[2,2,96,96]{3,2,1,0:T(8,128)}, u32[]{:S(2)}) %copy-start.6) | copy-done | bytes 147480
  8.9 0.0 copy-start.7
  8.9 0.9 %copy-done.7 = f32[192,192]{1,0:T(8,128)S(1)} copy-done((f32[192,192]{1,0:T(8,128)S(1)}, f32[192,192]{1,0:T(8,128)}, u32[]{:S(2)}) %copy-start.7) | copy-done | bytes 147480
  9.8 70.8 %shard_map.113 = (f32[2,2,96,96]{3,2,1,0:T(8,128)S(1)}, f32[2,192,192]{2,1,0:T(8,128)S(1)}) custom-call(s32[1,1,2,2]{3,2,1,0:T(2,128)S(1)} %copy-done.8, s32[1,1]{1,0:T(1,128)S(6)} %copy.14.counts, f32[2,2,96,96]{3,2,1,0:T(8,128)S(1)} %copy-done.6, f32[2,192,192]{2,1,0:T(8,128)S(1)} %copy-done.2, f32[192,192]{1,0:T(8,128)S(1)} %copy-done.7, ...), custom_call_target="tpu_custom_call" | custom-call | tf_op jit(solution)/shard_map/pallas_call | solution.py:510
  80.6 0.7 copy.15
  81.3 0.7 copy.16
Async XLA Ops:
  1.3 0.7 copy-start.8
  2.0 1.0 %copy-start = (bf16[512,512]{1,0:T(8,128)(2,1)S(1)}, bf16[512,512]{1,0:T(8,128)(2,1)}, u32[]{:S(2)}) copy-start(bf16[512,512]{1,0:T(8,128)(2,1)} %constant.9.clone.wrl) | copy-start | bytes 1572868
  3.0 1.0 %copy-start.1 = (bf16[512,512]{1,0:T(8,128)(2,1)S(1)}, bf16[512,512]{1,0:T(8,128)(2,1)}, u32[]{:S(2)}) copy-start(bf16[512,512]{1,0:T(8,128)(2,1)} %constant.8.clone.wrh) | copy-start | bytes 1572868
  4.0 1.0 %copy-start.2 = (f32[2,192,192]{2,1,0:T(8,128)S(1)}, f32[2,192,192]{2,1,0:T(8,128)}, u32[]{:S(2)}) copy-start(f32[2,192,192]{2,1,0:T(8,128)} %probe.1) | copy-start | bytes 884740
  5.0 1.0 %copy-start.3 = (f32[1,1,2,192,192]{4,3,2,1,0:T(8,128)S(1)}, f32[1,1,2,192,192]{4,3,2,1,0:T(8,128)}, u32[]{:S(2)}) copy-start(f32[1,1,2,192,192]{4,3,2,1,0:T(8,128)} %param.13) | copy-start | bytes 884740
  6.0 1.0 %copy-start.4 = (bf16[384,384]{1,0:T(8,128)(2,1)S(1)}, bf16[384,384]{1,0:T(8,128)(2,1)}, u32[]{:S(2)}) copy-start(bf16[384,384]{1,0:T(8,128)(2,1)} %constant.11.clone.wll) | copy-start | bytes 884740
  7.0 1.0 %copy-start.5 = (bf16[384,384]{1,0:T(8,128)(2,1)S(1)}, bf16[384,384]{1,0:T(8,128)(2,1)}, u32[]{:S(2)}) copy-start(bf16[384,384]{1,0:T(8,128)(2,1)} %constant.10.clone.wlh) | copy-start | bytes 884740
  8.0 0.9 %copy-start.6 = (f32[2,2,96,96]{3,2,1,0:T(8,128)S(1)}, f32[2,2,96,96]{3,2,1,0:T(8,128)}, u32[]{:S(2)}) copy-start(f32[2,2,96,96]{3,2,1,0:T(8,128)} %obj.1) | copy-start | bytes 442372
  8.9 0.9 %copy-start.7 = (f32[192,192]{1,0:T(8,128)S(1)}, f32[192,192]{1,0:T(8,128)}, u32[]{:S(2)}) copy-start(f32[192,192]{1,0:T(8,128)} %phase.1) | copy-start | bytes 442372

commit v2 on v1

--- a/solution.py
+++ b/solution.py
@@ -16,6 +16,7 @@
 LANES = 256
 SLOTS = 2
 HALF = 288
+PART = 48
 MESH = pl.DeviceIdType.MESH
 AROUND = [(i, j) for i in (-1, 0, 1) for j in (-1, 0, 1) if (i, j) != (0, 0)]
 F32 = jnp.float32
@@ -58,23 +59,43 @@
     return ar * br + ai * bi, ar * bi - ai * br
 
 
+def packed(a, b, c, d):
+    lane = lax.broadcasted_iota(jnp.int32, a.shape, 1)
+    b, c, d = pltpu.roll(b, 96, 1), pltpu.roll(c, 64, 1), pltpu.roll(d, 32, 1)
+    return jnp.where(lane < 96, a, b), jnp.where(lane < 64, b, c), jnp.where(lane < 32, c, d)
+
+
+def unpacked(u, v, w):
+    lane = lax.broadcasted_iota(jnp.int32, u.shape, 1)
+    b = jnp.where(lane < 32, pltpu.roll(u, 32, 1), pltpu.roll(v, 32, 1))
+    c = jnp.where(lane < 64, pltpu.roll(v, 64, 1), pltpu.roll(w, 64, 1))
+    return u, b, c, pltpu.roll(w, 96, 1)
+
+
 def dot(a, b):
     return jnp.dot(a, b, preferred_element_type=F32)
 
 
 def chunks(body, step, total=WIDTH):
-    def run(i, carry):
-        body(pl.multiple_of(i * step, step))
-        return carry
-
-    lax.fori_loop(0, total // step, run, 0)
+    for at in range(0, total, step):
+        body(at)
 
 
 def kernel(
     rows, cols, share, owners,
-    offsets, counts, obj, probe, phase, measured, wrh, wrl, wlh, wll,
+    offsets_in, counts_in, obj_in, probe_in, phase_in, measured_in, *rest,
+):
+    wide_in, (obj_out, probe_out), rest = rest[:4], rest[4:6], rest[6:]
+    fetch(rows, cols, share, owners, offsets_in, counts_in, obj_in, probe_in, phase_in,
+          measured_in, wide_in, obj_out, probe_out, *rest)
+
+
+def fetch(
+    rows, cols, share, owners,
+    offsets_in, counts_in, obj_in, probe_in, phase_in, measured_in, wide_in,
     obj_out, probe_out,
-    own, halo, band, win, wave, trans, xh, xl, lh, ll, y, carried, shift,
+    offsets, counts, obj, probe, phase, measured, wrh, wrl, wlh, wll, load,
+    wide, own, halo, band, win, wave, trans, xh, xl, lh, ll, y, carried, shift,
     gsend, grecv, pack, half_in, plane_in, deep_in, total,
     halo_s, halo_r, grad_s, grad_r, pair_s, pair_r, plane_s, plane_r, deep_s, deep_r,
     back_s, back_r, last_s, last_r,
@@ -101,6 +122,18 @@
     def inside(i, j):
         return (r + i >= 0) & (r + i < rows) & (c + j >= 0) & (c + j < cols)
 
+    loads = [
+        pltpu.make_async_copy(a, b, load.at[i])
+        for i, (a, b) in enumerate(
+            zip(
+                (obj_in, offsets_in, counts_in, probe_in, phase_in, *wide_in, measured_in.at[0, 0]),
+                (obj, offsets, counts, probe, phase, wrh, wrl, wlh, wll, measured),
+            )
+        )
+    ]
+    for one in loads:
+        one.start()
+
     barrier = pltpu.get_barrier_semaphore()
 
     def greet(device):
@@ -115,10 +148,15 @@
     for d in range(1, depth):
         greet((lax.rem(z + d, depth) * 4 + x_lo * 2 + core, c))
 
+    loads[0].wait()
     for s in range(2):
+        quarters = []
         for k in range(2):
-            own[s, k] = jnp.zeros((TILE, 128), F32)
-            own[s, k, :, :TILE] = obj[s, k]
+            wide[s, k] = jnp.zeros((TILE, 128), F32)
+            wide[s, k, :, :TILE] = obj[s, k]
+            quarters += [wide[s, k, :PART], wide[s, k, PART:]]
+        for m, v in enumerate(packed(*quarters)):
+            own[s, m] = v
 
     pl.semaphore_wait(barrier, len(AROUND) + group + depth - 1)
 
@@ -146,6 +184,8 @@
         for i, j in AROUND:
             halo_copy(s, i, j).start()
 
+    for one in loads[1:]:
+        one.wait()
     for k in range(2):
         wave[k] = jnp.zeros((WIDTH, LANES), F32)
         wave[k, :, :WIDTH] = probe[k]
@@ -163,22 +203,28 @@
     live = [slot < counts[0, 0] for slot in range(SLOTS)]
 
     def windows(s):
+        lane = lax.broadcasted_iota(jnp.int32, (PART, 128), 1)
         for i in (-1, 0, 1):
+            tiles = []
+            for j in (-1, 0, 1):
+                if (i, j) == (0, 0):
+                    tiles.append(unpacked(*[own[s, m] for m in range(3)]))
+                else:
+                    keep = inside(i, j)
+                    tiles.append(
+                        unpacked(
+                            *[jnp.where(keep, halo[s, place(i, j), m], 0.0) for m in range(3)]
+                        )
+                    )
             for k in range(2):
-                pieces = []
-                for j in (-1, 0, 1):
-                    if (i, j) == (0, 0):
-                        pieces.append(own[s, k])
-                    else:
-                        pieces.append(jnp.where(inside(i, j), halo[s, place(i, j), k], 0.0))
-                lane = lax.broadcasted_iota(jnp.int32, (TILE, 128), 1)
-                a = pieces[0]
-                b = pltpu.roll(pieces[1], 96, 1)
-                d = pltpu.roll(pieces[2], 64, 1)
-                at = pl.ds((i + 1) * TILE, TILE)
-                band[k, 0, at] = jnp.where(lane < 96, a, b)
-                band[k, 1, at] = jnp.where(lane < 64, b, d)
-                band[k, 2, at] = jnp.where(lane < 64, d, 0.0)
+                for h in range(2):
+                    a, b, d = [tile[2 * k + h] for tile in tiles]
+                    b = pltpu.roll(b, 96, 1)
+                    d = pltpu.roll(d, 64, 1)
+                    at = pl.ds((i + 1) * TILE + h * PART, PART)
+                    band[k, 0, at] = jnp.where(lane < 96, a, b)
+                    band[k, 1, at] = jnp.where(lane < 64, b, d)
+                    band[k, 2, at] = jnp.where(lane < 64, d, 0.0)
         for slot in range(SLOTS):
             for k in range(2):
                 lane = lax.broadcasted_iota(jnp.int32, (WIDTH, 128), 1)
@@ -219,25 +265,30 @@
             chunks(functools.partial(body, slot), step)
 
     def spread(s):
+        lane = lax.broadcasted_iota(jnp.int32, (PART, 128), 1)
         for i in (-1, 0, 1):
+            tiles = ([], [], [])
             for k in range(2):
-                lane = lax.broadcasted_iota(jnp.int32, (TILE, 128), 1)
-                v = [0.0, 0.0, 0.0]
-                for slot in range(SLOTS):
-                    at = pl.ds(TILE * (i + 2) - ro[slot], TILE)
-                    a = pltpu.roll(shift[slot, k, 0, at], co[slot], 1)
-                    b = pltpu.roll(shift[slot, k, 1, at], co[slot], 1)
-                    wrap = lane < co[slot]
-                    v[0] = v[0] + jnp.where(wrap, 0.0, a)
-                    v[1] = v[1] + jnp.where(wrap, a, b)
-                    v[2] = v[2] + jnp.where(wrap, b, 0.0)
-                gsend[s, place(i, -1), k] = v[0]
-                gsend[s, place(i, 0), k] = jnp.where(
-                    lane < 32, pltpu.roll(v[0], 32, 1), pltpu.roll(v[1], 32, 1)
-                )
-                gsend[s, place(i, 1), k] = jnp.where(
-                    lane < 64, pltpu.roll(v[1], 64, 1), pltpu.roll(v[2], 64, 1)
-                )
+                for h in range(2):
+                    v = [0.0, 0.0, 0.0]
+                    for slot in range(SLOTS):
+                        at = pl.ds(TILE * (i + 2) + PART * h - ro[slot], PART)
+                        a = pltpu.roll(shift[slot, k, 0, at], co[slot], 1)
+                        b = pltpu.roll(shift[slot, k, 1, at], co[slot], 1)
+                        wrap = lane < co[slot]
+                        v[0] = v[0] + jnp.where(wrap, 0.0, a)
+                        v[1] = v[1] + jnp.where(wrap, a, b)
+                        v[2] = v[2] + jnp.where(wrap, b, 0.0)
+                    tiles[0].append(v[0])
+                    tiles[1].append(
+                        jnp.where(lane < 32, pltpu.roll(v[0], 32, 1), pltpu.roll(v[1], 32, 1))
+                    )
+                    tiles[2].append(
+                        jnp.where(lane < 64, pltpu.roll(v[1], 64, 1), pltpu.roll(v[2], 64, 1))
+                    )
+            for j in (-1, 0, 1):
+                for m, part in enumerate(packed(*tiles[j + 1])):
+                    gsend[s, place(i, j), m] = part
 
     def shifted(slot, at, re, im):
         to = pl.ds(TILE + at, step)
@@ -372,11 +423,15 @@
         grad_copy(1, i, j).wait_recv()
 
     def update(s):
-        for k in range(2):
-            whole = gsend[s, place(0, 0), k]
+        sums = []
+        for m in range(3):
+            whole = gsend[s, place(0, 0), m]
             for i, j in AROUND:
-                whole = whole + jnp.where(inside(i, j), grecv[s, place(i, j), k], 0.0)
-            obj_out[s, k] = obj[s, k] - OBJECT_RATE * whole[:, :TILE]
+                whole = whole + jnp.where(inside(i, j), grecv[s, place(i, j), m], 0.0)
+            sums.append(whole)
+        for p, part in enumerate(unpacked(*sums)):
+            k, at = p // 2, pl.ds(p % 2 * PART, PART)
+            obj_out[s, k, at] = obj[s, k, at] - OBJECT_RATE * part[:, :TILE]
 
     update(1)
 
@@ -504,7 +559,6 @@
 
     def shards(object_slices, probe, propagator_phase, measured, offsets, counts):
         vmem = pl.BlockSpec(memory_space=pltpu.VMEM)
-        smem = pl.BlockSpec(memory_space=pltpu.SMEM)
         dma = pltpu.SemaphoreType.DMA
         square = (WIDTH, LANES)
         return pl.pallas_call(
@@ -513,11 +567,20 @@
                 jax.ShapeDtypeStruct(object_slices.shape, F32),
                 jax.ShapeDtypeStruct(probe.shape, F32),
             ),
-            in_specs=[smem, smem] + [vmem] * 8,
+            in_specs=[pl.BlockSpec(memory_space=pltpu.HBM)] * 10,
             out_specs=(vmem, vmem),
             scratch_shapes=[
+                pltpu.SMEM((1, 1, SLOTS, 2), jnp.int32),
+                pltpu.SMEM((1, 1), jnp.int32),
+                pltpu.VMEM(object_slices.shape, F32),
+                pltpu.VMEM(probe.shape, F32),
+                pltpu.VMEM(propagator_phase.shape, F32),
+                pltpu.VMEM(measured.shape[2:], F32),
+                *[pltpu.VMEM(m.shape, BF16) for m in consts],
+                dma((10,)),
                 pltpu.VMEM((2, 2, TILE, 128), F32),
-                pltpu.VMEM((2, 9, 2, TILE, 128), F32),
+                pltpu.VMEM((2, 3, PART, 128), F32),
+                pltpu.VMEM((2, 9, 3, PART, 128), F32),
                 pltpu.VMEM((2, 3, 3 * TILE, 128), F32),
                 pltpu.VMEM((2, SLOTS, 2) + square, F32),
                 pltpu.VMEM((2,) + square, F32),
@@ -529,8 +592,8 @@
                 pltpu.VMEM((SLOTS, 2 * WIDTH, LANES), F32),
                 pltpu.VMEM((SLOTS, 2) + square, F32),
                 pltpu.VMEM((SLOTS, 2, 2, 4 * TILE, 128), F32),
-                pltpu.VMEM((2, 9, 2, TILE, 128), F32),
-                pltpu.VMEM((2, 9, 2, TILE, 128), F32),
+                pltpu.VMEM((2, 9, 3, PART, 128), F32),
+                pltpu.VMEM((2, 9, 3, PART, 128), F32),
                 pltpu.VMEM((2 * HALF, 128), F32),
                 pltpu.VMEM((HALF, 128), F32),
                 pltpu.VMEM((group, share, 128), F32),
@@ -544,10 +607,10 @@
                 dma((owners,)), dma((owners,)),
             ],
             compiler_params=pltpu.CompilerParams(
-                collective_id=0, has_side_effects=True, vmem_limit_bytes=48 * 1024 * 1024
+                collective_id=0, has_side_effects=True, vmem_limit_bytes=62 * 1024 * 1024
             ),
         )(
-            offsets, counts, object_slices, probe, propagator_phase, measured[0, 0],
+            offsets, counts, object_slices, probe, propagator_phase, measured,
             *[jnp.asarray(m) for m in consts],
         )
 

time: 82.4 us -> 66.4 us (0.81)
  Pallas kernels: 70.8 us -> 62.6 us
  local copies, waits for them, and re-layouts: 9.94 us -> 2.42 us
    pallas_call x1, Pallas kernels: 70.8 us -> 62.6 us  [shards(): pl.pallas_call(functools.partial(kernel, rows, cols, share, owners), out_...]
    unnamed x20 -> x4, local copies, waits for them, and re-layouts: 9.94 us -> 2.42 us
where the time goes in v2:
time: 66.4 us; the launch traced here: 66.3 us
  Pallas kernels  62.6 us (94%)
  local copies, waits for them, and re-layouts  2.42 us (4%)
  between operations  1.29 us (2%)
    pallas_call x1, Pallas kernels, shards(): pl.pallas_call(functools.partial(kernel, rows, cols, share, owners), out_...  62.6 us
    unnamed x4, local copies, waits for them, and re-layouts  2.42 us

profile of v2, /device:TPU:1, one launch (start us, length us, event | category | flops | bytes accessed | tf_op | source)
XLA Modules:
  0.0 66.3 jit_solution(4130123925490575562)
XLA Ops:
  1.3 62.6 %shard_map.113 = (f32[2,2,96,96]{3,2,1,0:T(8,128)}, f32[2,192,192]{2,1,0:T(8,128)}) custom-call(s32[1,1,2,2]{3,2,1,0:T(2,128)} %offsets_in.1, s32[1,1]{1,0:T(1,128)S(6)} %copy.14.counts_in, f32[2,2,96,96]{3,2,1,0:T(8,128)} %obj_in.1, f32[2,192,192]{2,1,0:T(8,128)} %probe_in.1, f32[192,192]{1,0:T(8,128)} %phase_in.1, f32[1,1,2,192,192]{4,3,2,1,0:T(8,128)} %measured_in.1, ...), custom_call_target="tpu_custom_call" | custom-call | tf_op jit(solution)/shard_map/pallas_call | solution.py:564
  63.8 0.0 copy-start
  63.9 1.7 %copy.15 = f32[2,2,96,96]{3,2,1,0:T(8,128)} copy(f32[2,2,96,96]{3,2,1,0:T(8,128)} %get-tuple-element.4) | data formatting | bytes 294912
  65.5 0.0 copy-done
  65.5 0.7 %copy.16 = f32[2,192,192]{2,1,0:T(8,128)} copy(f32[2,192,192]{2,1,0:T(8,128)S(1)} %copy-done) | data formatting | bytes 589824
Async XLA Ops:
  63.8 1.7 %copy-start = (f32[2,192,192]{2,1,0:T(8,128)S(1)}, f32[2,192,192]{2,1,0:T(8,128)}, u32[]{:S(2)}) copy-start(f32[2,192,192]{2,1,0:T(8,128)} %get-tuple-element.5) | copy-start | bytes 884740

commit v3 on v2

--- a/solution.py
+++ b/solution.py
@@ -18,6 +18,7 @@
 HALF = 288
 PART = 48
 MESH = pl.DeviceIdType.MESH
+SIDES = (-1, 1)
 AROUND = [(i, j) for i in (-1, 0, 1) for j in (-1, 0, 1) if (i, j) != (0, 0)]
 F32 = jnp.float32
 BF16 = jnp.bfloat16
@@ -95,9 +96,9 @@
     offsets_in, counts_in, obj_in, probe_in, phase_in, measured_in, wide_in,
     obj_out, probe_out,
     offsets, counts, obj, probe, phase, measured, wrh, wrl, wlh, wll, load,
-    wide, own, halo, band, win, wave, trans, xh, xl, lh, ll, y, carried, shift,
-    gsend, grecv, pack, half_in, plane_in, deep_in, total,
-    halo_s, halo_r, grad_s, grad_r, pair_s, pair_r, plane_s, plane_r, deep_s, deep_r,
+    wide, halo, band, win, wave, trans, xh, xl, lh, ll, y, carried, shift,
+    gsend, grow, gcol, pack, half_in, plane_in, deep_in, total,
+    halo_s, halo_r, col_s, col_r, row_s, row_r, grow_s, grow_r, gcol_s, gcol_r, pair_s, pair_r, plane_s, plane_r, deep_s, deep_r,
     back_s, back_r, last_s, last_r,
 ):
     r = lax.axis_index("row")
@@ -156,33 +157,64 @@
             wide[s, k, :, :TILE] = obj[s, k]
             quarters += [wide[s, k, :PART], wide[s, k, PART:]]
         for m, v in enumerate(packed(*quarters)):
-            own[s, m] = v
+            halo[s, place(0, 0), m] = v
 
     pl.semaphore_wait(barrier, len(AROUND) + group + depth - 1)
 
-    def halo_copy(s, i, j):
-        return pltpu.make_async_remote_copy(
-            src_ref=own.at[s],
-            dst_ref=halo.at[s, place(-i, -j)],
-            send_sem=halo_s.at[s, place(i, j)],
-            recv_sem=halo_r.at[s, place(-i, -j)],
+    def halo_copy(i, j):
+        return pltpu.make_async_remote_copy(
+            src_ref=halo.at[0, place(0, 0)],
+            dst_ref=halo.at[0, place(-i, -j)],
+            send_sem=halo_s.at[place(i, j)],
+            recv_sem=halo_r.at[place(-i, -j)],
             device_id=beside(i, j),
             device_id_type=MESH,
         )
 
-    def grad_copy(s, i, j):
-        return pltpu.make_async_remote_copy(
-            src_ref=gsend.at[s, place(i, j)],
-            dst_ref=grecv.at[s, place(-i, -j)],
-            send_sem=grad_s.at[s, place(i, j)],
-            recv_sem=grad_r.at[s, place(-i, -j)],
-            device_id=beside(i, j),
-            device_id_type=MESH,
-        )
-
-    for s in range(2):
-        for i, j in AROUND:
-            halo_copy(s, i, j).start()
+    def col_copy(j):
+        return pltpu.make_async_remote_copy(
+            src_ref=halo.at[1, place(0, 0)],
+            dst_ref=halo.at[1, place(0, -j)],
+            send_sem=col_s.at[j + 1],
+            recv_sem=col_r.at[1 - j],
+            device_id=beside(0, j),
+            device_id_type=MESH,
+        )
+
+    def row_copy(i):
+        return pltpu.make_async_remote_copy(
+            src_ref=halo.at[1, pl.ds(place(0, -1), 3)],
+            dst_ref=halo.at[1, pl.ds(place(-i, -1), 3)],
+            send_sem=row_s.at[i + 1],
+            recv_sem=row_r.at[1 - i],
+            device_id=beside(i, 0),
+            device_id_type=MESH,
+        )
+
+    def grad_row(s, i):
+        return pltpu.make_async_remote_copy(
+            src_ref=gsend.at[s, pl.ds(place(i, -1), 3)],
+            dst_ref=grow.at[s, 1 - i],
+            send_sem=grow_s.at[s, i + 1],
+            recv_sem=grow_r.at[s, 1 - i],
+            device_id=beside(i, 0),
+            device_id_type=MESH,
+        )
+
+    def grad_col(s, j):
+        return pltpu.make_async_remote_copy(
+            src_ref=gsend.at[s, place(0, j)],
+            dst_ref=gcol.at[s, 1 - j],
+            send_sem=gcol_s.at[s, j + 1],
+            recv_sem=gcol_r.at[s, 1 - j],
+            device_id=beside(0, j),
+            device_id_type=MESH,
+        )
+
+    for i, j in AROUND:
+        halo_copy(i, j).start()
+    for j in SIDES:
+        col_copy(j).start()
 
     for one in loads[1:]:
         one.wait()
@@ -208,7 +240,7 @@
             tiles = []
             for j in (-1, 0, 1):
                 if (i, j) == (0, 0):
-                    tiles.append(unpacked(*[own[s, m] for m in range(3)]))
+                    tiles.append(unpacked(*[halo[s, place(0, 0), m] for m in range(3)]))
                 else:
                     keep = inside(i, j)
                     tiles.append(
@@ -298,7 +330,11 @@
             shift[slot, k, 1, to] = part[:, 128:]
 
     for i, j in AROUND:
-        halo_copy(0, i, j).wait_recv()
+        halo_copy(i, j).wait_recv()
+    for j in SIDES:
+        col_copy(j).wait_recv()
+    for i in SIDES:
+        row_copy(i).start()
     windows(0)
 
     def enter(slot, at):
@@ -318,8 +354,8 @@
     each(carry)
     transform()
 
-    for i, j in AROUND:
-        halo_copy(1, i, j).wait_recv()
+    for i in SIDES:
+        row_copy(i).wait_recv()
     windows(1)
 
     def leave(slot, at):
@@ -353,8 +389,8 @@
 
     each(second)
     spread(1)
-    for i, j in AROUND:
-        grad_copy(1, i, j).start()
+    for i in SIDES:
+        grad_row(1, i).start()
     transform()
 
     def inner(slot, at):
@@ -398,8 +434,19 @@
     pair.start()
 
     spread(0)
-    for i, j in AROUND:
-        grad_copy(0, i, j).start()
+
+    def fold(s):
+        for i in SIDES:
+            grad_row(s, i).wait_recv()
+        for j in (-1, 1, 0):
+            for m in range(3):
+                whole = gsend[s, place(0, j), m]
+                for i in SIDES:
+                    keep = (r + i >= 0) & (r + i < rows)
+                    whole = whole + jnp.where(keep, grow[s, i + 1, j + 1, m], 0.0)
+                gsend[s, place(0, j), m] = whole
+            if j != 0:
+                grad_col(s, j).start()
 
     pair.wait_recv()
     half_in[...] = half_in[...] + pack[pl.ds(mine, HALF)]
@@ -419,21 +466,23 @@
         def _():
             plane_copy(q, me).start()
 
-    for i, j in AROUND:
-        grad_copy(1, i, j).wait_recv()
+    fold(1)
+    for i in SIDES:
+        grad_row(0, i).start()
 
     def update(s):
+        for j in SIDES:
+            grad_col(s, j).wait_recv()
         sums = []
         for m in range(3):
             whole = gsend[s, place(0, 0), m]
-            for i, j in AROUND:
-                whole = whole + jnp.where(inside(i, j), grecv[s, place(i, j), m], 0.0)
+            for j in SIDES:
+                keep = (c + j >= 0) & (c + j < cols)
+                whole = whole + jnp.where(keep, gcol[s, j + 1, m], 0.0)
             sums.append(whole)
         for p, part in enumerate(unpacked(*sums)):
             k, at = p // 2, pl.ds(p % 2 * PART, PART)
             obj_out[s, k, at] = obj[s, k, at] - OBJECT_RATE * part[:, :TILE]
-
-    update(1)
 
     my_share = pl.multiple_of(me * share, 8)
 
@@ -464,9 +513,8 @@
             def _():
                 deep_copy(k, z).start()
 
-    for i, j in AROUND:
-        grad_copy(0, i, j).wait_recv()
-    update(0)
+    fold(0)
+    update(1)
 
     def back_copy(p, sender):
         at = pl.ds(pl.multiple_of(mine + sender * share, 8), share)
@@ -505,6 +553,8 @@
             def _():
                 back_copy(p, me).start()
 
+    update(0)
+
     for q in range(owners):
         @pl.when(me != q)
         def _():
@@ -527,10 +577,14 @@
 
     chunks(finish, step)
 
-    for s in range(2):
-        for i, j in AROUND:
-            halo_copy(s, i, j).wait_send()
-            grad_copy(s, i, j).wait_send()
+    for i, j in AROUND:
+        halo_copy(i, j).wait_send()
+    for i in SIDES:
+        col_copy(i).wait_send()
+        row_copy(i).wait_send()
+        for s in range(2):
+            grad_row(s, i).wait_send()
+            grad_col(s, i).wait_send()
     pair.wait_send()
     for q in range(owners):
         @pl.when(me != q)
@@ -579,7 +633,6 @@
                 *[pltpu.VMEM(m.shape, BF16) for m in consts],
                 dma((10,)),
                 pltpu.VMEM((2, 2, TILE, 128), F32),
-                pltpu.VMEM((2, 3, PART, 128), F32),
                 pltpu.VMEM((2, 9, 3, PART, 128), F32),
                 pltpu.VMEM((2, 3, 3 * TILE, 128), F32),
                 pltpu.VMEM((2, SLOTS, 2) + square, F32),
@@ -593,13 +646,16 @@
                 pltpu.VMEM((SLOTS, 2) + square, F32),
                 pltpu.VMEM((SLOTS, 2, 2, 4 * TILE, 128), F32),
                 pltpu.VMEM((2, 9, 3, PART, 128), F32),
-                pltpu.VMEM((2, 9, 3, PART, 128), F32),
+                pltpu.VMEM((2, 3, 3, 3, PART, 128), F32),
+                pltpu.VMEM((2, 3, 3, PART, 128), F32),
                 pltpu.VMEM((2 * HALF, 128), F32),
                 pltpu.VMEM((HALF, 128), F32),
                 pltpu.VMEM((group, share, 128), F32),
                 pltpu.VMEM((depth, share, 128), F32),
                 pltpu.VMEM((2 * HALF, 128), F32),
-                dma((2, 9)), dma((2, 9)), dma((2, 9)), dma((2, 9)),
+                dma((9,)), dma((9,)),
+                dma((3,)), dma((3,)), dma((3,)), dma((3,)),
+                dma((2, 3)), dma((2, 3)), dma((2, 3)), dma((2, 3)),
                 dma, dma,
                 dma((owners,)), dma((group,)),
                 dma((depth,)), dma((depth,)),

time: 66.4 us -> 61.9 us (0.932)
  Pallas kernels: 62.6 us -> 58.1 us
    pallas_call x1, Pallas kernels: 62.6 us -> 58.1 us  [shards(): pl.pallas_call(functools.partial(kernel, rows, cols, share, owners), out_...]
where the time goes in v3:
time: 61.9 us; the launch traced here: 61.8 us
  Pallas kernels  58.1 us (94%)
  local copies, waits for them, and re-layouts  2.42 us (4%)
  between operations  1.29 us (2%)
    pallas_call x1, Pallas kernels, shards(): pl.pallas_call(functools.partial(kernel, rows, cols, share, owners), out_...  58.1 us
    unnamed x4, local copies, waits for them, and re-layouts  2.42 us

profile of v3, /device:TPU:1, one launch (start us, length us, event | category | flops | bytes accessed | tf_op | source)
XLA Modules:
  0.0 61.8 jit_solution(18140872369997945420)
XLA Ops:
  1.3 58.1 %shard_map.113 = (f32[2,2,96,96]{3,2,1,0:T(8,128)}, f32[2,192,192]{2,1,0:T(8,128)}) custom-call(s32[1,1,2,2]{3,2,1,0:T(2,128)} %offsets_in.1, s32[1,1]{1,0:T(1,128)S(6)} %copy.14.counts_in, f32[2,2,96,96]{3,2,1,0:T(8,128)} %obj_in.1, f32[2,192,192]{2,1,0:T(8,128)} %probe_in.1, f32[192,192]{1,0:T(8,128)} %phase_in.1, f32[1,1,2,192,192]{4,3,2,1,0:T(8,128)} %measured_in.1, ...), custom_call_target="tpu_custom_call" | custom-call | tf_op jit(solution)/shard_map/pallas_call | solution.py:618
  59.3 0.0 copy-start
  59.3 1.7 %copy.15 = f32[2,2,96,96]{3,2,1,0:T(8,128)} copy(f32[2,2,96,96]{3,2,1,0:T(8,128)} %get-tuple-element.4) | data formatting | bytes 294912
  61.0 0.0 copy-done
  61.0 0.7 %copy.16 = f32[2,192,192]{2,1,0:T(8,128)} copy(f32[2,192,192]{2,1,0:T(8,128)S(1)} %copy-done) | data formatting | bytes 589824
Async XLA Ops:
  59.3 1.7 %copy-start = (f32[2,192,192]{2,1,0:T(8,128)S(1)}, f32[2,192,192]{2,1,0:T(8,128)}, u32[]{:S(2)}) copy-start(f32[2,192,192]{2,1,0:T(8,128)} %get-tuple-element.5) | copy-start | bytes 884740

commit v4 on v3

--- a/solution.py
+++ b/solution.py
@@ -19,7 +19,7 @@
 PART = 48
 MESH = pl.DeviceIdType.MESH
 SIDES = (-1, 1)
-AROUND = [(i, j) for i in (-1, 0, 1) for j in (-1, 0, 1) if (i, j) != (0, 0)]
+AROUND = [(-1, -1), (-1, 1), (1, -1), (1, 1), (0, -1), (0, 1), (-1, 0), (1, 0)]
 F32 = jnp.float32
 BF16 = jnp.bfloat16
 
@@ -44,7 +44,7 @@
         high = full.astype(np.float32).astype(ml_dtypes.bfloat16)
         low = (full - high.astype(np.float64)).astype(np.float32).astype(ml_dtypes.bfloat16)
         parts += [high, low]
-    return parts
+    return parts[:2] + [np.concatenate([parts[2], parts[2], parts[3]], axis=1)]
 
 
 def two(x):
@@ -86,7 +86,7 @@
     rows, cols, share, owners,
     offsets_in, counts_in, obj_in, probe_in, phase_in, measured_in, *rest,
 ):
-    wide_in, (obj_out, probe_out), rest = rest[:4], rest[4:6], rest[6:]
+    wide_in, (obj_out, probe_out), rest = rest[:3], rest[3:5], rest[5:]
     fetch(rows, cols, share, owners, offsets_in, counts_in, obj_in, probe_in, phase_in,
           measured_in, wide_in, obj_out, probe_out, *rest)
 
@@ -95,8 +95,8 @@
     rows, cols, share, owners,
     offsets_in, counts_in, obj_in, probe_in, phase_in, measured_in, wide_in,
     obj_out, probe_out,
-    offsets, counts, obj, probe, phase, measured, wrh, wrl, wlh, wll, load,
-    wide, halo, band, win, wave, trans, xh, xl, lh, ll, y, carried, shift,
+    offsets, counts, obj, probe, phase, measured, wrh, wrl, wl, load,
+    wide, halo, band, win, wave, trans, xh, xl, lh, y, carried, shift,
     gsend, grow, gcol, pack, half_in, plane_in, deep_in, total,
     halo_s, halo_r, col_s, col_r, row_s, row_r, grow_s, grow_r, gcol_s, gcol_r, pair_s, pair_r, plane_s, plane_r, deep_s, deep_r,
     back_s, back_r, last_s, last_r,
@@ -128,7 +128,7 @@
         for i, (a, b) in enumerate(
             zip(
                 (obj_in, offsets_in, counts_in, probe_in, phase_in, *wide_in, measured_in.at[0, 0]),
-                (obj, offsets, counts, probe, phase, wrh, wrl, wlh, wll, measured),
+                (obj, offsets, counts, probe, phase, wrh, wrl, wl, measured),
             )
         )
     ]
@@ -211,10 +211,10 @@
             device_id_type=MESH,
         )
 
+    for j in SIDES:
+        col_copy(j).start()
     for i, j in AROUND:
         halo_copy(i, j).start()
-    for j in SIDES:
-        col_copy(j).start()
 
     for one in loads[1:]:
         one.wait()
@@ -278,12 +278,13 @@
         acc = dot(xh[...], wrh[...]) + dot(xl[...], wrh[...]) + dot(xh[...], wrl[...])
         for slot in range(SLOTS):
             part = acc[slot * WIDTH : (slot + 1) * WIDTH]
-            lh[slot, :WIDTH], ll[slot, :WIDTH] = two(part[:, :LANES])
-            lh[slot, WIDTH:], ll[slot, WIDTH:] = two(part[:, LANES:])
+            for k in range(2):
+                high, low = two(part[:, k * LANES : (k + 1) * LANES])
+                for m, piece in enumerate((high, low, high)):
+                    at = 2 * m * WIDTH + k * WIDTH
+                    lh[slot, at : at + WIDTH] = piece
         for slot in range(SLOTS):
-            y[slot] = (
-                dot(wlh[...], lh[slot]) + dot(wlh[...], ll[slot]) + dot(wll[...], lh[slot])
-            )
+            y[slot] = dot(wl[...], lh[slot])
 
     def got(slot, at, step, inverse):
         one = y[slot, pl.ds(at, step), :]
@@ -329,12 +330,12 @@
             shift[slot, k, 0, to] = part[:, :128]
             shift[slot, k, 1, to] = part[:, 128:]
 
-    for i, j in AROUND:
-        halo_copy(i, j).wait_recv()
     for j in SIDES:
         col_copy(j).wait_recv()
     for i in SIDES:
         row_copy(i).start()
+    for i, j in AROUND:
+        halo_copy(i, j).wait_recv()
     windows(0)
 
     def enter(slot, at):
@@ -621,7 +622,7 @@
                 jax.ShapeDtypeStruct(object_slices.shape, F32),
                 jax.ShapeDtypeStruct(probe.shape, F32),
             ),
-            in_specs=[pl.BlockSpec(memory_space=pltpu.HBM)] * 10,
+            in_specs=[pl.BlockSpec(memory_space=pltpu.HBM)] * 9,
             out_specs=(vmem, vmem),
             scratch_shapes=[
                 pltpu.SMEM((1, 1, SLOTS, 2), jnp.int32),
@@ -631,7 +632,7 @@
                 pltpu.VMEM(propagator_phase.shape, F32),
                 pltpu.VMEM(measured.shape[2:], F32),
                 *[pltpu.VMEM(m.shape, BF16) for m in consts],
-                dma((10,)),
+                dma((9,)),
                 pltpu.VMEM((2, 2, TILE, 128), F32),
                 pltpu.VMEM((2, 9, 3, PART, 128), F32),
                 pltpu.VMEM((2, 3, 3 * TILE, 128), F32),
@@ -640,8 +641,7 @@
                 pltpu.VMEM((2,) + square, F32),
                 pltpu.VMEM((SLOTS * WIDTH, 2 * LANES), BF16),
                 pltpu.VMEM((SLOTS * WIDTH, 2 * LANES), BF16),
-                pltpu.VMEM((SLOTS, 2 * WIDTH, LANES), BF16),
-                pltpu.VMEM((SLOTS, 2 * WIDTH, LANES), BF16),
+                pltpu.VMEM((SLOTS, 6 * WIDTH, LANES), BF16),
                 pltpu.VMEM((SLOTS, 2 * WIDTH, LANES), F32),
                 pltpu.VMEM((SLOTS, 2) + square, F32),
                 pltpu.VMEM((SLOTS, 2, 2, 4 * TILE, 128), F32),
@@ -663,11 +663,15 @@
                 dma((owners,)), dma((owners,)),
             ],
             compiler_params=pltpu.CompilerParams(
-                collective_id=0, has_side_effects=True, vmem_limit_bytes=62 * 1024 * 1024
+                collective_id=0, has_side_effects=True, vmem_limit_bytes=48 * 1024 * 1024
             ),
         )(
-            offsets, counts, object_slices, probe, propagator_phase, measured,
-            *[jnp.asarray(m) for m in consts],
+            pltpu.with_memory_space_constraint(offsets, pltpu.HBM), counts,
+            *[
+                pltpu.with_memory_space_constraint(x, pltpu.HBM)
+                for x in (object_slices, probe, propagator_phase, measured)
+            ],
+            *[pltpu.with_memory_space_constraint(jnp.asarray(m), pltpu.HBM) for m in consts],
         )
 
     return jax.shard_map(

time: 61.9 us -> 58.7 us (0.948)
  Pallas kernels: 58.1 us -> 55.8 us
  local copies, waits for them, and re-layouts: 2.42 us -> 1.42 us
    pallas_call x1, Pallas kernels: 58.1 us -> 55.8 us  [shards(): pl.pallas_call(functools.partial(kernel, rows, cols, share, owners), out_...]
    unnamed x4 -> x2, local copies, waits for them, and re-layouts: 2.42 us -> 1.42 us
where the time goes in v4:
time: 58.7 us; the launch traced here: 58.5 us
  Pallas kernels  55.8 us (95%)
  local copies, waits for them, and re-layouts  1.42 us (2%)
  between operations  1.29 us (2%)
    pallas_call x1, Pallas kernels, shards(): pl.pallas_call(functools.partial(kernel, rows, cols, share, owners), out_...  55.8 us
    unnamed x2, local copies, waits for them, and re-layouts  1.42 us

profile of v4, /device:TPU:1, one launch (start us, length us, event | category | flops | bytes accessed | tf_op | source)
XLA Modules:
  0.0 58.5 jit_solution(16606021786460284155)
XLA Ops:
  1.3 55.8 %shard_map.104 = (f32[2,2,96,96]{3,2,1,0:T(8,128)S(1)}, f32[2,192,192]{2,1,0:T(8,128)S(1)}) custom-call(s32[1,1,2,2]{3,2,1,0:T(2,128)} %offsets_in.1, s32[1,1]{1,0:T(1,128)S(6)} %copy.13.counts_in, f32[2,2,96,96]{3,2,1,0:T(8,128)} %obj_in.1, f32[2,192,192]{2,1,0:T(8,128)} %probe_in.1, f32[192,192]{1,0:T(8,128)} %phase_in.1, ...), custom_call_target="tpu_custom_call" | custom-call | tf_op jit(solution)/shard_map/pallas_call | solution.py:619
  57.1 0.7 %copy.14 = f32[2,2,96,96]{3,2,1,0:T(8,128)} copy(f32[2,2,96,96]{3,2,1,0:T(8,128)S(1)} %get-tuple-element.4) | data formatting | bytes 294912
  57.8 0.7 %copy.15 = f32[2,192,192]{2,1,0:T(8,128)} copy(f32[2,192,192]{2,1,0:T(8,128)S(1)} %get-tuple-element.5) | data formatting | bytes 589824

commit v5 on v4

--- a/solution.py
+++ b/solution.py
@@ -412,7 +412,6 @@
             pr, pi = times_conj(win[0, slot, 0, d], win[0, slot, 1, d], ir, ii)
             re = re + jnp.where(live[slot], pr, 0.0)
             im = im + jnp.where(live[slot], pi, 0.0)
-            shifted(slot, at, *times_conj(wave[0, d], wave[1, d], ir, ii))
         lane = lax.broadcasted_iota(jnp.int32, (step, 128), 1)
         pack[d] = re[:, :128]
         pack[pl.ds(WIDTH + at, step)] = im[:, :128]
@@ -434,7 +433,11 @@
     )
     pair.start()
 
-    spread(0)
+    def first(slot, at):
+        d = pl.ds(at, step)
+        shifted(slot, at, *times_conj(wave[0, d], wave[1, d], *got(slot, at, step, True)))
+
+    each(first)
 
     def fold(s):
         for i in SIDES:
@@ -467,6 +470,7 @@
         def _():
             plane_copy(q, me).start()
 
+    spread(0)
     fold(1)
     for i in SIDES:
         grad_row(0, i).start()

time: 58.7 us -> 57.6 us (0.981)
  Pallas kernels: 55.8 us -> 54.8 us
    pallas_call x1, Pallas kernels: 55.8 us -> 54.8 us  [shards(): pl.pallas_call(functools.partial(kernel, rows, cols, share, owners), out_...]
where the time goes in v5:
time: 57.6 us; the launch traced here: 57.5 us
  Pallas kernels  54.8 us (95%)
  local copies, waits for them, and re-layouts  1.42 us (2%)
  between operations  1.29 us (2%)
    pallas_call x1, Pallas kernels, shards(): pl.pallas_call(functools.partial(kernel, rows, cols, share, owners), out_...  54.8 us
    unnamed x2, local copies, waits for them, and re-layouts  1.42 us

profile of v5, /device:TPU:1, one launch (start us, length us, event | category | flops | bytes accessed | tf_op | source)
XLA Modules:
  0.0 57.5 jit_solution(16949166232183019417)
XLA Ops:
  1.3 54.8 %shard_map.104 = (f32[2,2,96,96]{3,2,1,0:T(8,128)S(1)}, f32[2,192,192]{2,1,0:T(8,128)S(1)}) custom-call(s32[1,1,2,2]{3,2,1,0:T(2,128)} %offsets_in.1, s32[1,1]{1,0:T(1,128)S(6)} %copy.13.counts_in, f32[2,2,96,96]{3,2,1,0:T(8,128)} %obj_in.1, f32[2,192,192]{2,1,0:T(8,128)} %probe_in.1, f32[192,192]{1,0:T(8,128)} %phase_in.1, ...), custom_call_target="tpu_custom_call" | custom-call | tf_op jit(solution)/shard_map/pallas_call | solution.py:623
  56.1 0.7 %copy.14 = f32[2,2,96,96]{3,2,1,0:T(8,128)} copy(f32[2,2,96,96]{3,2,1,0:T(8,128)S(1)} %get-tuple-element.4) | data formatting | bytes 294912
  56.8 0.7 %copy.15 = f32[2,192,192]{2,1,0:T(8,128)} copy(f32[2,192,192]{2,1,0:T(8,128)S(1)} %get-tuple-element.5) | data formatting | bytes 589824

commit v6 on v5

--- a/solution.py
+++ b/solution.py
@@ -275,9 +275,9 @@
         xh[to, LANES:], xl[to, LANES:] = two(im)
 
     def transform():
-        acc = dot(xh[...], wrh[...]) + dot(xl[...], wrh[...]) + dot(xh[...], wrl[...])
         for slot in range(SLOTS):
-            part = acc[slot * WIDTH : (slot + 1) * WIDTH]
+            d = slice(slot * WIDTH, (slot + 1) * WIDTH)
+            part = dot(xh[d], wrh[...]) + dot(xl[d], wrh[...]) + dot(xh[d], wrl[...])
             for k in range(2):
                 high, low = two(part[:, k * LANES : (k + 1) * LANES])
                 for m, piece in enumerate((high, low, high)):

time: 57.6 us -> 57.2 us (level)
  no operation moved by 1% of the time
where the time goes in v6:
time: 57.2 us; the launch traced here: 57 us
  Pallas kernels  54.3 us (95%)
  local copies, waits for them, and re-layouts  1.42 us (2%)
  between operations  1.29 us (2%)
    pallas_call x1, Pallas kernels, shards(): pl.pallas_call(functools.partial(kernel, rows, cols, share, owners), out_...  54.3 us
    unnamed x2, local copies, waits for them, and re-layouts  1.42 us

profile of v6, /device:TPU:1, one launch (start us, length us, event | category | flops | bytes accessed | tf_op | source)
XLA Modules:
  0.0 57.0 jit_solution(1753986881219787687)
XLA Ops:
  1.3 54.3 %shard_map.104 = (f32[2,2,96,96]{3,2,1,0:T(8,128)S(1)}, f32[2,192,192]{2,1,0:T(8,128)S(1)}) custom-call(s32[1,1,2,2]{3,2,1,0:T(2,128)} %offsets_in.1, s32[1,1]{1,0:T(1,128)S(6)} %copy.13.counts_in, f32[2,2,96,96]{3,2,1,0:T(8,128)} %obj_in.1, f32[2,192,192]{2,1,0:T(8,128)} %probe_in.1, f32[192,192]{1,0:T(8,128)} %phase_in.1, ...), custom_call_target="tpu_custom_call" | custom-call | tf_op jit(solution)/shard_map/pallas_call | solution.py:623
  55.6 0.7 %copy.14 = f32[2,2,96,96]{3,2,1,0:T(8,128)} copy(f32[2,2,96,96]{3,2,1,0:T(8,128)S(1)} %get-tuple-element.4) | data formatting | bytes 294912
  56.3 0.7 %copy.15 = f32[2,192,192]{2,1,0:T(8,128)} copy(f32[2,192,192]{2,1,0:T(8,128)S(1)} %get-tuple-element.5) | data formatting | bytes 589824
